TPU v7x, 32 devices: a whole 2x2x4 slice. The times are simulated.
32 devices in a mesh: dp: 8 (over y, x, core), mp: 4 (over z).
Axes of the slice: x: 2, y: 2, z: 4, core: 2. Of those that a mesh axis runs over, the one named last changes fastest.
Arguments:
- gradients: bfloat16 [8, 40, 512, 512], P('dp', 'mp'), may hold values from -16 to 16
- factor_state: float32 [4, 8, 2, 2, 512, 512], P('mp', 'dp'), as said below
- block_owner: int32 [4, 10], P('mp'), may hold values from 0 to 7, as said below
Outputs:
- directions: bfloat16 [40, 512, 512], P('mp')
- next_state: float32 [4, 8, 2, 2, 512, 512], P('mp', 'dp')
Inputs may be any that keep to these rules, and one draw needn't show every extreme that they name: `block_owner`: within one row (one index of mp) no owner appears more than 2 times, and some owner appears exactly 2 times. Every index of dp owns some block. `factor_state`: every factor matrix is symmetric positive definite.
All inputs are finite; a program needn't handle non-finite values.
Results may differ from a plain program's by a relative error of at most 0.0004.
Values may be sent and summed in bfloat16 or wider, within the bound.
A program may use at most 128 MiB of HBM per device.

v0:
```python
import jax
import jax.numpy as jnp
from jax import lax
from jax.sharding import PartitionSpec as P

SLOTS = 2
ITERS = 3


decay_rate = 0.95
ridge_term = 0.001
tiny_offset = 1e-06


def product(left, right):
    return jnp.dot(left, right, precision=lax.Precision.HIGHEST)


def inverse_root(matrix):
    width_rows = matrix.shape[0]
    identity = jnp.eye(width_rows, dtype=matrix.dtype)
    shifted = matrix + ridge_term * identity
    level_norm = jnp.sqrt(jnp.sum(shifted * shifted))
    moving = shifted / level_norm
    result = identity * level_norm ** (-0.25)
    for turn_index in range(ITERS):
        factor = (5.0 * identity - moving) * 0.25
        result = product(result, factor)
        if turn_index + 1 < ITERS:
            square = product(factor, factor)
            fourth = product(square, square)
            moving = product(fourth, moving)
    return result


def maybe_root(occupied, matrix):
    return lax.cond(occupied, inverse_root, jnp.zeros_like, matrix)


def grafted(gradient, left_root, right_root):
    precond = product(product(left_root, gradient), right_root)
    target = jnp.sqrt(jnp.mean(gradient * gradient) + tiny_offset)
    actual = jnp.sqrt(jnp.mean(precond * precond) + tiny_offset)
    return precond * (target / actual)


def owner_slots(owners):
    block_count = owners.shape[0]
    positions = jnp.arange(block_count, dtype=jnp.int32)
    same_owner = owners[:, None] == owners[None, :]
    earlier = positions[None, :] < positions[:, None]
    return jnp.sum((same_owner & earlier).astype(jnp.int32), axis=1)


def clip_factor(mean_square):
    return 1.0 / jnp.sqrt(mean_square + tiny_offset)


def shards(gradients, factor_state, block_owner):
    owners = block_owner[0]
    slot_of = owner_slots(owners)
    positions = jnp.arange(owners.shape[0], dtype=jnp.int32)
    myself = lax.axis_index("dp")
    local_terms = gradients[0].astype(jnp.float32)
    entries = local_terms.size * lax.axis_size("mp")
    summed = lax.psum(local_terms, "dp")
    square_sum = lax.psum(jnp.sum(summed * summed), "mp")
    clipped = summed * clip_factor(square_sum / entries)
    chosen = []
    for holding_slot_index in range(SLOTS):
        matches = (owners == myself) & (slot_of == holding_slot_index)
        chosen.append((jnp.any(matches), jnp.sum(jnp.where(matches, positions, 0))))
    lefts = []
    rights = []
    blocks_held = []
    pairs = []
    for slot_index in range(SLOTS):
        occupied, block_index = chosen[slot_index]
        gradient = lax.dynamic_index_in_dim(clipped, block_index, 0, keepdims=False)
        old_pair = factor_state[0, 0, slot_index]
        left = decay_rate * old_pair[0] + (1.0 - decay_rate) * product(gradient, gradient.T)
        right = decay_rate * old_pair[1] + (1.0 - decay_rate) * product(gradient.T, gradient)
        lefts.append(left)
        rights.append(right)
        blocks_held.append(gradient)
        pairs.append(jnp.where(occupied, jnp.stack([left, right]), old_pair))
    next_state = jnp.stack(pairs)[None, None]
    left_roots = [
        maybe_root(chosen[slot_index][0], lefts[slot_index]) for slot_index in range(SLOTS)
    ]
    right_roots = [
        maybe_root(chosen[slot_index][0], rights[slot_index]) for slot_index in range(SLOTS)
    ]
    finished = []
    for slot_index in range(SLOTS):
        finished.append(
            grafted(
                blocks_held[slot_index], left_roots[slot_index], right_roots[slot_index]
            ).astype(jnp.bfloat16)
        )
    canvas = jnp.zeros(clipped.shape, jnp.bfloat16)
    for slot_index in range(SLOTS):
        occupied, block_index = chosen[slot_index]
        current = lax.dynamic_index_in_dim(canvas, block_index, 0, keepdims=False)
        update = jnp.where(occupied, finished[slot_index], current)
        canvas = lax.dynamic_update_index_in_dim(canvas, update, block_index, 0)
    directions = lax.psum(canvas, "dp").astype(jnp.float32).astype(jnp.bfloat16)
    return (directions, next_state)


def solution(mesh):
    in_specs = (P("dp", "mp", None, None), P("mp", "dp", None, None, None, None), P("mp", None))
    out_specs = (P("mp", None, None), P("mp", "dp", None, None, None, None))
    return jax.shard_map(shards, mesh=mesh, in_specs=in_specs, out_specs=out_specs, check_vma=False)
```

profile of v0, /device:TPU:0, one launch (start us, length us, event | category | flops | bytes accessed | tf_op | source)
XLA Modules:
  0.0 445.1 jit_solution(650618435341468626)
XLA Ops:
  7.2 0.0 all-reduce.3.cloned.1.call-start
  7.2 7.8 %bitcast_convert_fusion = f32[10,512,512]{2,1,0:T(8,128)} fusion(bf16[1,10,512,512]{3,2,1,0:T(8,128)(2,1)} %param.11), kind=kLoop, calls=%fused_computation.165 | loop fusion | flops 2621440 | bytes 15728640 | tf_op jit(solution)/shard_map/convert_element_type | solution.py:64
  15.0 0.0 all-reduce.3.cloned.1.call-update
  15.0 0.0 all-reduce.5.cloned.1.call-start
  15.1 0.6 copy-done.12
  15.6 0.2 convert_reduce_fusion
  15.8 0.7 fusion.201
  16.5 0.6 select_reduce_fusion
  21.6 145.6 %all-reduce.3.cloned.1.call-done = f32[10,512,512]{2,1,0:T(8,128)} async-done(((f32[10,512,512]{2,1,0:T(8,128)}), f32[10,512,512]{2,1,0:T(8,128)}) %all-reduce.3.cloned.1.call-update) | async-done | bytes 10485776 | tf_op jit(solution)/shard_map/psum | solution.py:66
  167.2 7.3 %multiply_reduce_fusion.4 = f32[]{:T(128)} fusion(f32[10,512,512]{2,1,0:T(8,128)} %all-reduce.3.cloned.1.call-done), kind=kLoop, calls=%fused_computation.164 | loop fusion | flops 5242879 | bytes 10485764 | tf_op jit(solution)/shard_map/reduce_sum | solution.py:67
  175.2 12.7 %psum.22 = f32[]{:T(128)} all-reduce(f32[]{:T(128)} %multiply_reduce_fusion.4), channel_id=1, replica_groups=mesh['dp'=8,'mp'=4] {'mp'}, use_global_device_ids=true, to_apply=%region_4.0 | all-reduce | flops 1 | bytes 8 | tf_op jit(solution)/shard_map/psum | solution.py:67
  188.5 6.0 %broadcast_multiply_fusion = f32[10,512,512]{2,1,0:T(8,128)S(1)} fusion(f32[10,512,512]{2,1,0:T(8,128)} %all-reduce.3.cloned.1.call-done, f32[]{:T(128)S(6)} %sqrt.27), kind=kLoop, calls=%fused_computation.166 | loop fusion | flops 2621440 | bytes 20971524 | tf_op jit(solution)/shard_map/mul | solution.py:68
  194.6 0.0 copy-start
  194.6 0.0 copy-start.2
  194.6 4.0 fusion.169
  198.7 4.4 fusion.168
  203.1 2.9 fusion.170
  206.0 2.9 fusion.171
  208.8 0.9 fusion.176
  209.7 10.2 %conditional.6 = (f32[512,512]{1,0:T(8,128)S(1)}) conditional(s32[]{:T(128)} %convert_element_type.34, () %tuple.34, f32[512,512]{1,0:T(8,128)S(1)} %fusion.169), branch_computations={%region_16.17_spmd, %region_17.19_spmd} | conditional | flops 14505213952 | bytes 28311628 | solution.py:37
  209.7 0.1 broadcast.88
  219.9 4.0 fusion.173
  223.9 10.9 %conditional.7 = (f32[512,512]{1,0:T(8,128)}) conditional(s32[]{:T(128)} %convert_element_type.34, () %tuple.35, f32[512,512]{1,0:T(8,128)S(1)} %fusion.168), branch_computations={%region_19.20_spmd, %region_20.22_spmd} | conditional | flops 14505213952 | bytes 28311628 | solution.py:37
  223.9 1.2 broadcast.93
  234.9 0.0 copy-start.5
  234.9 5.0 %multiply_reduce_fusion.5 = (f32[]{:T(128)}, f32[512,512]{1,0:T(8,128)}) fusion(f32[512,512]{1,0:T(8,128)} %fusion.173, f32[512,512]{1,0:T(8,128)} %get-tuple-element.39), kind=kOutput, calls=%fused_computation.191 | convolution fusion | flops 1611137024 | bytes 3145732 | tf_op jit(solution)/shard_map/dot_general | solution.py:16
  241.1 28.6 %conditional.4 = (f32[512,512]{1,0:T(8,128)S(1)}) conditional(s32[]{:T(128)} %convert_element_type.30, () %tuple.32, f32[512,512]{1,0:T(8,128)S(1)} %copy-done.5), branch_computations={%region_6.7_spmd, %region_7.0_spmd} | conditional | flops 14505213952 | bytes 32505960 | solution.py:37
  241.2 0.0 copy-start.6
  241.2 0.9 multiply_reduce_fusion
  242.7 2.0 fusion.10
  244.7 1.8 fusion.203
  246.6 3.1 fusion.39
  249.7 1.9 fusion.6
  251.6 1.8 fusion.204
  253.5 2.9 fusion
  256.5 3.7 fusion.3
  260.1 1.9 fusion.8
  262.1 1.8 fusion.205
  269.7 4.0 fusion.178
  273.7 24.4 %conditional.5 = (f32[512,512]{1,0:T(8,128)S(1)}) conditional(s32[]{:T(128)} %convert_element_type.30, () %tuple.33, f32[512,512]{1,0:T(8,128)} %fusion.170), branch_computations={%region_9.10_spmd, %region_10.12_spmd} | conditional | flops 14505213952 | bytes 32505960 | solution.py:37
  273.7 2.1 multiply_reduce_fusion.1
  276.5 3.7 fusion.52
  280.2 1.8 fusion.206
  282.1 1.9 fusion.81
  284.0 1.9 fusion.48
  285.9 1.8 fusion.207
  287.8 2.8 fusion.42
  290.7 0.0 copy-start.10
  290.7 3.4 fusion.45
  294.1 1.9 fusion.50
  296.0 1.8 fusion.208
  298.1 4.7 %multiply_reduce_fusion.6 = (f32[]{:T(128)}, f32[512,512]{1,0:T(8,128)}) fusion(f32[512,512]{1,0:T(8,128)} %fusion.178, f32[512,512]{1,0:T(8,128)S(1)} %get-tuple-element.37), kind=kOutput, calls=%fused_computation.193 | convolution fusion | flops 1611137024 | bytes 3145732 | tf_op jit(solution)/shard_map/dot_general | solution.py:16
  304.1 0.4 broadcast_in_dim.18
  304.6 0.8 copy-done.11
  305.3 0.8 fusion.190
  306.2 0.0 copy-start.1
  306.2 2.3 copy-done.1
  308.5 0.8 constant_dynamic-slice_fusion
  309.3 2.9 fusion.193
  312.3 0.0 all-reduce.5.cloned.1.call-update
  312.3 4.8 %maximum_select_fusion = (f32[1,2,512,512]{3,2,1,0:T(8,128)S(1)}, f32[1,2,512,512]{3,2,1,0:T(8,128)S(1)}) fusion(f32[1,1,512,512]{3,2,1,0:T(8,128)S(1)} %bitcast.104, f32[1,1,512,512]{3,2,1,0:T(8,128)} %bitcast.105, f32[1,1,2,2,512,512]{5,4,3,2,1,0:T(8,128)} %param.12, pred[]{:T(512)} %get-tuple-element.26, f32[1,1,512,512]{3,2,1,0:T(8,128)S(1)} %bitcast.103, ...), kind=kLoop, calls=%fused_computation.168 | loop fusion | flops 2097152 | bytes 12582914 | tf_op jit(solution)/shard_map/jit(_where)/select_n | solution.py:86
  317.1 2.5 maximum_bitcast_fusion
  319.5 113.3 %all-reduce.5.cloned.1.call-done = bf16[10,512,512]{2,1,0:T(8,128)(2,1)} async-done(((bf16[10,512,512]{2,1,0:T(8,128)(2,1)}), bf16[10,512,512]{2,1,0:T(8,128)(2,1)}) %all-reduce.5.cloned.1.call-update) | async-done | bytes 5242896 | tf_op jit(solution)/shard_map/psum | solution.py:107
  432.8 5.2 %copy.17 = bf16[10,512,512]{2,1,0:T(8,128)(2,1)} copy(bf16[10,512,512]{2,1,0:T(8,128)(2,1)} %all-reduce.5.cloned.1.call-done) | data formatting | bytes 10485760
  (13 shorter events, 0.0 us)
Async XLA Ops:
  7.2 160.1 %all-reduce.3.cloned.1.call-start = ((), (), s32[]{:S(2)}) async-start(), calls=%async_computation | async-start | bytes 20971520 | tf_op jit(solution)/shard_map/psum | solution.py:66
  15.0 0.7 copy-start.12
  15.0 417.8 %all-reduce.5.cloned.1.call-start = ((), (), s32[]{:S(2)}) async-start(), calls=%async_computation.1 | async-start | bytes 10485760 | tf_op jit(solution)/shard_map/psum | solution.py:107
  194.6 14.2 %copy-start = (f32[10,512,512]{2,1,0:T(8,128)}, f32[10,512,512]{2,1,0:T(8,128)S(1)}, u32[]{:S(2)}) copy-start(f32[10,512,512]{2,1,0:T(8,128)S(1)} %broadcast_multiply_fusion) | copy-start | bytes 31457284
  194.6 8.5 %copy-start.2 = (f32[1,1,2,2,512,512]{5,4,3,2,1,0:T(8,128)S(1)}, f32[1,1,2,2,512,512]{5,4,3,2,1,0:T(8,128)}, u32[]{:S(2)}) copy-start(f32[1,1,2,2,512,512]{5,4,3,2,1,0:T(8,128)} %param.12) | copy-start | bytes 12582916
  234.9 6.2 %copy-start.5 = (f32[512,512]{1,0:T(8,128)S(1)}, f32[512,512]{1,0:T(8,128)}, u32[]{:S(2)}) copy-start(f32[512,512]{1,0:T(8,128)} %fusion.171) | copy-start | bytes 3145732
  241.2 3.6 copy-start.6
  256.4 5.6 %copy-start.9 = (f32[512,512]{1,0:T(8,128)S(1)}, f32[512,512]{1,0:T(8,128)}, u32[]{:S(2)}) copy-start(f32[512,512]{1,0:T(8,128)} %fusion) | copy-start | bytes 3145732 | tf_op jit(solution)/shard_map/cond
  276.5 5.6 %copy-start.4 = (f32[512,512]{1,0:T(8,128)S(1)}, f32[512,512]{1,0:T(8,128)}, u32[]{:S(2)}) copy-start(f32[512,512]{1,0:T(8,128)} %param.3) | copy-start | bytes 3145732 | tf_op jit(solution)/shard_map/cond
  290.7 5.4 %copy-start.10 = (f32[512,512]{1,0:T(8,128)S(1)}, f32[512,512]{1,0:T(8,128)}, u32[]{:S(2)}) copy-start(f32[512,512]{1,0:T(8,128)} %fusion.42) | copy-start | bytes 3145732 | tf_op jit(solution)/shard_map/cond
  304.1 1.2 copy-start.11
  305.3 7.0 %copy-start.3 = (f32[512,512]{1,0:T(8,128)S(1)}, f32[512,512]{1,0:T(8,128)}, u32[]{:S(2)}) copy-start(f32[512,512]{1,0:T(8,128)} %fusion.170) | copy-start | bytes 3145732
  306.2 2.4 copy-start.1
Sparse Core Ops, SparseCore 0:
  15.1 152.0 all-reduce.2
  312.4 120.3 all-reduce.4
where the time goes:
time: 448 us; the launch traced here: 445 us
  waiting for transfers between devices  259 us (58%)
  matrix products  74.2 us (17%)
  other arithmetic  37.5 us (8%)
  loops' own time  27.5 us (6%)
  between operations  22.7 us (5%)
  blocking collectives  12.7 us (3%)
  local copies, waits for them, and re-layouts  11.5 us (3%)
    psum x1, waiting for transfers between devices, shards(): summed = lax.psum(local_terms, 'dp')  146 us
    psum x1, waiting for transfers between devices, shards(): directions = lax.psum(canvas, 'dp').astype(jnp.float32).astype(jnp.bfloat16)  113 us
    dot_general x26, matrix products, product(): return jnp.dot(left, right, precision=lax.Precision.HIGHEST)  74.2 us
    another operation x4, loops' own time, maybe_root(): return lax.cond(occupied, inverse_root, jnp.zeros_like, matrix)  27.5 us
    psum x1, blocking collectives, shards(): square_sum = lax.psum(jnp.sum(summed * summed), 'mp')  12.7 us
  transfers between devices with their start and end apart: 2, of which 2 were waited for; matrix products, arithmetic and copies ran while one was open for 2% of the time, Pallas kernels for 0%

commit v1 on v0

v1 whole, which is shorter than its diff:
```python
import functools

import jax
import jax.numpy as jnp
from jax import lax
from jax.experimental import pallas as pl
from jax.experimental.pallas import tpu as pltpu
from jax.sharding import PartitionSpec as P

ITERS = 3

decay_rate = 0.95
ridge_term = 0.001
tiny_offset = 1e-06

MESH = pl.DeviceIdType.MESH


def halves(value):
    high = value.astype(jnp.bfloat16)
    return high, (value - high.astype(jnp.float32)).astype(jnp.bfloat16)


def split_dot(left, right, dims=(1, 0)):
    def dot(a, b):
        return lax.dot_general(
            a, b, (((dims[0],), (dims[1],)), ((), ())), preferred_element_type=jnp.float32
        )
    return (dot(left[1], right[0]) + dot(left[0], right[1])) + dot(left[0], right[0])


def total_of(value):
    return jnp.sum(jnp.sum(value, axis=0, keepdims=True), axis=1, keepdims=True)


def inverse_root(matrix):
    width = matrix.shape[0]
    rows = lax.broadcasted_iota(jnp.int32, (width, width), 0)
    columns = lax.broadcasted_iota(jnp.int32, (width, width), 1)
    diagonal = rows == columns
    shifted = matrix + jnp.where(diagonal, ridge_term, 0.0)
    level_norm = jnp.sqrt(total_of(shifted * shifted))
    moving = shifted / level_norm
    result = None
    for turn in range(ITERS):
        factor = jnp.where(diagonal, 1.25, 0.0) - 0.25 * moving
        pair = halves(factor)
        result = factor if result is None else split_dot(halves(result), pair)
        if turn + 1 < ITERS:
            square = halves(split_dot(pair, pair))
            fourth = halves(split_dot(square, square))
            moving = split_dot(fourth, halves(moving))
    return result * (1.0 / jnp.sqrt(jnp.sqrt(level_norm)))


def step_kernel(n, n_mp, entries, keep_ref, sent_ref, state_ref, gathered_ref, next_ref,
                own, landed, summed, roots, finished, part, parts, row_part, row_parts,
                own_sem, send_sem, recv_sem, part_send, part_recv, row_send, row_recv,
                place_sem, out_send, out_recv, pair_send, pair_recv):
    me, mp = lax.axis_index("dp"), lax.axis_index("mp")
    slots, width = own.shape[0], own.shape[1]
    peers = [(k, lax.rem(me + k, n)) for k in range(1, n)]
    rows = [(k, lax.rem(mp + k, n_mp)) for k in range(1, n_mp)]

    barrier = pltpu.get_barrier_semaphore()
    for _, peer in peers:
        pl.semaphore_signal(barrier, inc=1, device_id=(peer, mp), device_id_type=MESH)
    for _, peer in rows:
        pl.semaphore_signal(barrier, inc=1, device_id=(me, peer), device_id_type=MESH)
    pl.semaphore_wait(barrier, n - 1 + n_mp - 1)

    copies = []
    for s in range(slots):
        group = []
        for k, peer in peers:
            copy = pltpu.make_async_remote_copy(
                src_ref=sent_ref.at[peer, s], dst_ref=landed.at[s, k - 1],
                send_sem=send_sem.at[s, k - 1], recv_sem=recv_sem.at[s, k - 1],
                device_id=(peer, mp), device_id_type=MESH)
            copy.start()
            group.append(copy)
        local = pltpu.make_async_copy(sent_ref.at[me, s], own.at[s], own_sem.at[s])
        local.start()
        copies.append((group, local))

    chunk = 64
    squares = []
    for s in range(slots):
        group, local = copies[s]
        local.wait()
        for copy in group:
            copy.wait_recv()

        def add(step, total):
            at = pl.ds(pl.multiple_of(step * chunk, chunk), chunk)
            value = own[s, at, :].astype(jnp.float32)
            for k in range(n - 1):
                value = value + landed[s, k, at, :].astype(jnp.float32)
            summed[s, at, :] = value
            return total + jnp.sum((value * value).reshape(chunk // 8, 8, width), axis=0)

        squares.append(total_of(lax.fori_loop(
            0, width // chunk, add, jnp.zeros((8, width), jnp.float32))))
        pair = halves(summed[s])
        next_ref[s, 0] = split_dot(pair, pair, (1, 1))
        next_ref[s, 1] = split_dot(pair, pair, (0, 0))

    part[...] = jnp.broadcast_to(functools.reduce(jnp.add, squares), part.shape)
    copies_part = []
    for k, peer in peers:
        copy = pltpu.make_async_remote_copy(
            src_ref=part, dst_ref=parts.at[k - 1], send_sem=part_send.at[k - 1],
            recv_sem=part_recv.at[k - 1], device_id=(peer, mp), device_id_type=MESH)
        copy.start()
        copies_part.append(copy)
    for copy in copies_part:
        copy.wait_recv()
    row_part[...] = part[...] + jnp.sum(parts[...], axis=0)
    copies_row = []
    for k, peer in rows:
        copy = pltpu.make_async_remote_copy(
            src_ref=row_part, dst_ref=row_parts.at[k - 1], send_sem=row_send.at[k - 1],
            recv_sem=row_recv.at[k - 1], device_id=(me, peer), device_id_type=MESH)
        copy.start()
        copies_row.append(copy)
    for copy in copies_row:
        copy.wait_recv()
    total = row_part[...] + jnp.sum(row_parts[...], axis=0)
    clip = (1.0 / jnp.sqrt(total / entries + tiny_offset))[:1, :1]

    core, pairs = lax.rem(me, 2), n // 2
    place = me // 2

    def out_copies(s):
        found = []
        for j in range(1, pairs):
            peer = lax.rem(place + j, pairs) * 2 + core
            found.append(pltpu.make_async_remote_copy(
                src_ref=finished.at[s], dst_ref=gathered_ref.at[me, s],
                send_sem=out_send.at[s, j], recv_sem=out_recv.at[s, j],
                device_id=(peer, mp), device_id_type=MESH))
        return found

    def pair_copy(s, j):
        source = lax.rem(place - j + pairs, pairs) * 2 + core
        return pltpu.make_async_remote_copy(
            src_ref=finished.at[s] if j == 0 else gathered_ref.at[source, s],
            dst_ref=gathered_ref.at[source, s],
            send_sem=pair_send.at[s, j], recv_sem=pair_recv.at[s, j],
            device_id=(me + 1 - 2 * core, mp), device_id_type=MESH)

    def place_copy(s):
        return pltpu.make_async_copy(finished.at[s], gathered_ref.at[me, s], place_sem.at[s])

    size = width * width
    for s in range(slots):

        def side_turn(side, carry):
            fresh = keep_ref[s] * state_ref[s, side] + (
                (1.0 - decay_rate) * clip * clip) * next_ref[s, side]
            next_ref[s, side] = fresh
            roots[side] = inverse_root(fresh)
            return carry

        lax.fori_loop(0, 2, side_turn, 0)
        gradient = summed[s] * clip
        precond = split_dot(halves(roots[0]), halves(gradient))
        precond = split_dot(halves(precond), halves(roots[1]))
        target = jnp.sqrt(squares[s] * clip * clip / size + tiny_offset)
        actual = jnp.sqrt(total_of(precond * precond) / size + tiny_offset)
        finished[s] = (precond * (target / actual)).astype(jnp.bfloat16)
        for copy in out_copies(s):
            copy.start()
        pair_copy(s, 0).start()
        place_copy(s).start()

    for s in range(slots):
        for j, copy in enumerate(out_copies(s)):
            copy.wait_recv()
            pair_copy(s, j + 1).start()
    for s in range(slots):
        for copy in out_copies(s):
            copy.wait_send()
        for j in range(pairs):
            pair_copy(s, j).wait()
        place_copy(s).wait()
        for copy in copies[s][0]:
            copy.wait_send()
    for copy in copies_part + copies_row:
        copy.wait_send()


def place_kernel(index_ref, valid_ref, source_ref, target_ref):
    value = source_ref[...].astype(jnp.float32)
    valid = valid_ref[pl.program_id(0)] > 0
    target_ref[...] = jnp.where(valid, value, 0.0).astype(target_ref.dtype)


def placed(source, index, valid):
    count, shape = index.shape[0], source.shape[1:]
    moved = 2 * count * shape[0] * shape[1] * source.dtype.itemsize
    return pl.pallas_call(
        place_kernel,
        out_shape=jax.ShapeDtypeStruct((count,) + shape, source.dtype),
        grid_spec=pltpu.PrefetchScalarGridSpec(
            num_scalar_prefetch=2, grid=(count,),
            in_specs=[pl.BlockSpec((1,) + shape, lambda i, index, valid: (index[i], 0, 0))],
            out_specs=pl.BlockSpec((1,) + shape, lambda i, index, valid: (i, 0, 0))),
        cost_estimate=pl.CostEstimate(flops=0, bytes_accessed=moved, transcendentals=0),
    )(index, valid, source)


def owner_slots(owners):
    positions = jnp.arange(owners.shape[0], dtype=jnp.int32)
    same_owner = owners[:, None] == owners[None, :]
    earlier = positions[None, :] < positions[:, None]
    return jnp.sum((same_owner & earlier).astype(jnp.int32), axis=1)


def shards(n, n_mp, gradients, factor_state, block_owner):
    owners = block_owner[0]
    blocks, width = gradients.shape[1], gradients.shape[2]
    slots = factor_state.shape[2]
    slot_of = owner_slots(owners)
    positions = jnp.arange(blocks, dtype=jnp.int32)
    spot = owners * slots + slot_of
    hits = jnp.arange(n * slots, dtype=jnp.int32)[:, None] == spot[None, :]
    occupied = jnp.any(hits, axis=1)
    block_at = jnp.sum(jnp.where(hits, positions[None, :], 0), axis=1)
    sent = placed(gradients[0], block_at, occupied.astype(jnp.int32))
    sent = sent.reshape(n, slots, width, width)
    mine = lax.dynamic_slice_in_dim(occupied, lax.axis_index("dp") * slots, slots)
    keep = jnp.where(mine, decay_rate, 1.0).astype(jnp.float32)

    vmem, sem = pltpu.VMEM, pltpu.SemaphoreType.DMA
    f32, bf16 = jnp.float32, jnp.bfloat16
    entries = float(blocks * n_mp * width * width)
    pairs = n // 2
    gathered, fresh = pl.pallas_call(
        functools.partial(step_kernel, n, n_mp, entries),
        out_shape=(jax.ShapeDtypeStruct((n, slots, width, width), bf16),
                   jax.ShapeDtypeStruct(factor_state.shape[2:], f32)),
        in_specs=[pl.BlockSpec(memory_space=pltpu.SMEM), pl.BlockSpec(memory_space=pl.ANY),
                  pl.BlockSpec(memory_space=vmem)],
        out_specs=(pl.BlockSpec(memory_space=pl.ANY), pl.BlockSpec(memory_space=vmem)),
        scratch_shapes=[
            vmem((slots, width, width), bf16), vmem((slots, n - 1, width, width), bf16),
            vmem((slots, width, width), f32), vmem((2, width, width), f32),
            vmem((slots, width, width), bf16),
            vmem((8, 128), f32), vmem((n - 1, 8, 128), f32),
            vmem((8, 128), f32), vmem((n_mp - 1, 8, 128), f32),
            sem((slots,)), sem((slots, n - 1)), sem((slots, n - 1)),
            sem((n - 1,)), sem((n - 1,)), sem((n_mp - 1,)), sem((n_mp - 1,)),
            sem((slots,)), sem((slots, pairs)), sem((slots, pairs)),
            sem((slots, pairs)), sem((slots, pairs))],
        compiler_params=pltpu.CompilerParams(
            collective_id=0, has_side_effects=True, vmem_limit_bytes=62 * 1024 * 1024),
    )(keep, sent, factor_state[0, 0])
    directions = placed(
        gathered.reshape(n * slots, width, width), spot, jnp.ones((blocks,), jnp.int32))
    return (directions, fresh[None, None])


def solution(mesh):
    in_specs = (P("dp", "mp", None, None), P("mp", "dp", None, None, None, None), P("mp", None))
    out_specs = (P("mp", None, None), P("mp", "dp", None, None, None, None))
    body = functools.partial(shards, mesh.shape["dp"], mesh.shape["mp"])
    return jax.shard_map(body, mesh=mesh, in_specs=in_specs, out_specs=out_specs, check_vma=False)
```

time: 448 us -> 209 us (0.47)
  waiting for transfers between devices: 259 us -> 0 us
  Pallas kernels: 0 us -> 199 us
  matrix products: 74.2 us -> 0 us
  other arithmetic: 37.5 us -> 3.91 us
  loops' own time: 27.5 us -> 0 us
  between operations: 22.7 us -> 0.66 us
  blocking collectives: 12.7 us -> 0 us
  local copies, waits for them, and re-layouts: 11.5 us -> 5.23 us
    psum x2 -> x0, waiting for transfers between devices: 259 us -> none  [the longest x1 146 us: shards(): summed = lax.psum(local_terms, 'dp')]
    pallas_call x0 -> x3, Pallas kernels: none -> 199 us  [the longest x1 177 us: shards(): pl.pallas_call(functools.partial(step_kernel, n, n_mp, entries), out_shap...]
    dot_general x26 -> x0, matrix products: 74.2 us -> none  [product(): return jnp.dot(left, right, precision=lax.Precision.HIGHEST)]
    another operation x4 -> x0, loops' own time: 27.5 us -> none  [maybe_root(): return lax.cond(occupied, inverse_root, jnp.zeros_like, matrix)]
    psum x1 -> x0, blocking collectives: 12.7 us -> none  [shards(): square_sum = lax.psum(jnp.sum(summed * summed), 'mp')]
    reduce_sum x5 -> x1, other arithmetic: 11.8 us -> 0.63 us  [shards(): block_at = jnp.sum(jnp.where(hits, positions[None, :], 0), axis=1)]
    convert_element_type x1, other arithmetic: 7.77 us -> 0.48 us  [shards(): sent = placed(gradients[0], block_at, occupied.astype(jnp.int32))]
    mul x1 -> x0, other arithmetic: 6.05 us -> none  [shards(): clipped = summed * clip_factor(square_sum / entries)]
  transfers between devices with their start and end apart: 2 -> 0, of which waited for: 2 -> 0; matrix products, arithmetic and copies ran while one was open for 2% -> 0% of each run, Pallas kernels for 0% -> 0%
where the time goes in v1:
time: 209 us; the launch traced here: 208 us
  Pallas kernels  199 us (95%)
  local copies, waits for them, and re-layouts  5.23 us (3%)
  other arithmetic  3.91 us (2%)
    pallas_call x1, Pallas kernels, shards(): pl.pallas_call(functools.partial(step_kernel, n, n_mp, entries), out_shap...  177 us
    pallas_call x2, Pallas kernels, placed(): pl.pallas_call(place_kernel, out_shape=jax.ShapeDtypeStruct((count,) + sh...  21.8 us
    unnamed x3, local copies, waits for them, and re-layouts  4.64 us

profile of v1, /device:TPU:0, one launch (start us, length us, event | category | flops | bytes accessed | tf_op | source)
XLA Modules:
  0.0 208.4 jit_solution(6872654694940756478)
XLA Ops:
  0.6 0.9 convert_reduce_fusion
  1.5 0.7 fusion.2
  2.2 0.1 fusion
  2.3 0.6 dynamic-slice_select_fusion.keep_ref
  2.9 0.5 convert_element_type.7.valid_ref
  3.4 0.6 select_reduce_fusion.index_ref
  4.0 12.9 %shard_map.50 = bf16[16,512,512]{2,1,0:T(8,128)(2,1)} custom-call(s32[16]{0:T(128)} %select_reduce_fusion.index_ref, s32[16]{0:T(128)} %convert_element_type.7.valid_ref, bf16[10,512,512]{2,1,0:T(8,128)(2,1)} %bitcast.15), custom_call_target="tpu_custom_call" | custom-call | bytes 16777216 | tf_op jit(solution)/shard_map/pallas_call | solution.py:202
  17.0 0.0 copy-start
  17.0 176.9 %shard_map.51 = (bf16[8,2,512,512]{3,2,1,0:T(8,128)(2,1)}, f32[2,2,512,512]{3,2,1,0:T(8,128)}) custom-call(f32[2]{0:T(128)} %dynamic-slice_select_fusion.keep_ref, bf16[8,2,512,512]{3,2,1,0:T(8,128)(2,1)} %bitcast.13, f32[2,2,512,512]{3,2,1,0:T(8,128)} %bitcast.16), custom_call_target="tpu_custom_call" | custom-call | tf_op jit(solution)/shard_map/pallas_call | solution.py:239
  193.8 0.0 copy-done
  193.8 0.5 multiply_add_fusion.index_ref
  194.4 0.6 broadcast_2_valid_ref.2.valid_ref
  195.0 8.8 %shard_map.52 = bf16[10,512,512]{2,1,0:T(8,128)(2,1)} custom-call(s32[10]{0:T(128)} %multiply_add_fusion.index_ref, s32[10]{0:T(128)} %broadcast_2_valid_ref.2.valid_ref, bf16[16,512,512]{2,1,0:T(8,128)(2,1)} %bitcast.14), custom_call_target="tpu_custom_call" | custom-call | bytes 10485760 | tf_op jit(solution)/shard_map/pallas_call | solution.py:202
  203.8 4.6 %copy.6 = f32[1,1,2,2,512,512]{5,4,3,2,1,0:T(8,128)} copy(f32[1,1,2,2,512,512]{5,4,3,2,1,0:T(8,128)} %bitcast.17) | data formatting | bytes 8388608
Async XLA Ops:
  17.0 176.9 %copy-start = (s32[1,10]{1,0:T(1,128)S(1)}, s32[1,10]{1,0:T(1,128)}, u32[]{:S(2)}) copy-start(s32[1,10]{1,0:T(1,128)} %param.5) | copy-start | bytes 124

commit v2 on v1

--- a/solution.py
+++ b/solution.py
@@ -191,9 +191,15 @@
 
 
 def place_kernel(index_ref, valid_ref, source_ref, target_ref):
-    value = source_ref[...].astype(jnp.float32)
     valid = valid_ref[pl.program_id(0)] > 0
-    target_ref[...] = jnp.where(valid, value, 0.0).astype(target_ref.dtype)
+
+    @pl.when(valid)
+    def _():
+        target_ref[...] = source_ref[...]
+
+    @pl.when(jnp.logical_not(valid))
+    def _():
+        target_ref[...] = jnp.zeros_like(target_ref)
 
 
 def placed(source, index, valid):

time: 209 us -> 209 us (level)
  no operation moved by 1% of the time
where the time goes in v2:
time: 209 us; the launch traced here: 208 us
  Pallas kernels  198 us (95%)
  local copies, waits for them, and re-layouts  5.23 us (3%)
  other arithmetic  3.91 us (2%)
    pallas_call x1, Pallas kernels, shards(): pl.pallas_call(functools.partial(step_kernel, n, n_mp, entries), out_shap...  177 us
    pallas_call x2, Pallas kernels, placed(): pl.pallas_call(place_kernel, out_shape=jax.ShapeDtypeStruct((count,) + sh...  21.2 us
    unnamed x3, local copies, waits for them, and re-layouts  4.64 us

profile of v2, /device:TPU:0, one launch (start us, length us, event | category | flops | bytes accessed | tf_op | source)
XLA Modules:
  0.0 207.6 jit_solution(9755083257183222525)
XLA Ops:
  0.6 0.9 convert_reduce_fusion
  1.5 0.7 fusion.2
  2.2 0.1 fusion
  2.3 0.6 dynamic-slice_select_fusion.keep_ref
  2.9 0.5 convert_element_type.7.valid_ref
  3.4 0.6 select_reduce_fusion.index_ref
  4.0 12.6 %shard_map.50 = bf16[16,512,512]{2,1,0:T(8,128)(2,1)} custom-call(s32[16]{0:T(128)} %select_reduce_fusion.index_ref, s32[16]{0:T(128)} %convert_element_type.7.valid_ref, bf16[10,512,512]{2,1,0:T(8,128)(2,1)} %bitcast.15), custom_call_target="tpu_custom_call" | custom-call | bytes 16777216 | tf_op jit(solution)/shard_map/pallas_call | solution.py:208
  16.6 0.0 copy-start
  16.6 176.6 %shard_map.51 = (bf16[8,2,512,512]{3,2,1,0:T(8,128)(2,1)}, f32[2,2,512,512]{3,2,1,0:T(8,128)}) custom-call(f32[2]{0:T(128)} %dynamic-slice_select_fusion.keep_ref, bf16[8,2,512,512]{3,2,1,0:T(8,128)(2,1)} %bitcast.13, f32[2,2,512,512]{3,2,1,0:T(8,128)} %bitcast.16), custom_call_target="tpu_custom_call" | custom-call | tf_op jit(solution)/shard_map/pallas_call | solution.py:245
  193.3 0.0 copy-done
  193.3 0.5 multiply_add_fusion.index_ref
  193.8 0.6 broadcast_2_valid_ref.2.valid_ref
  194.4 8.6 %shard_map.52 = bf16[10,512,512]{2,1,0:T(8,128)(2,1)} custom-call(s32[10]{0:T(128)} %multiply_add_fusion.index_ref, s32[10]{0:T(128)} %broadcast_2_valid_ref.2.valid_ref, bf16[16,512,512]{2,1,0:T(8,128)(2,1)} %bitcast.14), custom_call_target="tpu_custom_call" | custom-call | bytes 10485760 | tf_op jit(solution)/shard_map/pallas_call | solution.py:208
  203.0 4.6 %copy.6 = f32[1,1,2,2,512,512]{5,4,3,2,1,0:T(8,128)} copy(f32[1,1,2,2,512,512]{5,4,3,2,1,0:T(8,128)} %bitcast.17) | data formatting | bytes 8388608
Async XLA Ops:
  16.6 176.6 %copy-start = (s32[1,10]{1,0:T(1,128)S(1)}, s32[1,10]{1,0:T(1,128)}, u32[]{:S(2)}) copy-start(s32[1,10]{1,0:T(1,128)} %param.5) | copy-start | bytes 124

commit v3 on v2

--- a/solution.py
+++ b/solution.py
@@ -33,28 +33,31 @@
     return jnp.sum(jnp.sum(value, axis=0, keepdims=True), axis=1, keepdims=True)
 
 
-def inverse_root(matrix):
-    width = matrix.shape[0]
+def inverse_roots(matrices):
+    width = matrices[0].shape[0]
     rows = lax.broadcasted_iota(jnp.int32, (width, width), 0)
     columns = lax.broadcasted_iota(jnp.int32, (width, width), 1)
     diagonal = rows == columns
-    shifted = matrix + jnp.where(diagonal, ridge_term, 0.0)
-    level_norm = jnp.sqrt(total_of(shifted * shifted))
-    moving = shifted / level_norm
+    shifted = [matrix + jnp.where(diagonal, ridge_term, 0.0) for matrix in matrices]
+    level_norm = [jnp.sqrt(total_of(each * each)) for each in shifted]
+    moving = [each / norm for each, norm in zip(shifted, level_norm)]
     result = None
     for turn in range(ITERS):
-        factor = jnp.where(diagonal, 1.25, 0.0) - 0.25 * moving
-        pair = halves(factor)
-        result = factor if result is None else split_dot(halves(result), pair)
+        factor = [jnp.where(diagonal, 1.25, 0.0) - 0.25 * each for each in moving]
+        pair = [halves(each) for each in factor]
+        if result is None:
+            result = factor
+        else:
+            result = [split_dot(halves(x), p) for x, p in zip(result, pair)]
         if turn + 1 < ITERS:
-            square = halves(split_dot(pair, pair))
-            fourth = halves(split_dot(square, square))
-            moving = split_dot(fourth, halves(moving))
-    return result * (1.0 / jnp.sqrt(jnp.sqrt(level_norm)))
+            square = [halves(split_dot(p, p)) for p in pair]
+            fourth = [halves(split_dot(q, q)) for q in square]
+            moving = [split_dot(f, halves(m)) for f, m in zip(fourth, moving)]
+    return [x * (1.0 / jnp.sqrt(jnp.sqrt(norm))) for x, norm in zip(result, level_norm)]
 
 
 def step_kernel(n, n_mp, entries, keep_ref, sent_ref, state_ref, gathered_ref, next_ref,
-                own, landed, summed, roots, finished, part, parts, row_part, row_parts,
+                own, landed, summed, finished, part, parts, row_part, row_parts,
                 own_sem, send_sem, recv_sem, part_send, part_recv, row_send, row_recv,
                 place_sem, out_send, out_recv, pair_send, pair_recv):
     me, mp = lax.axis_index("dp"), lax.axis_index("mp")
@@ -155,17 +158,16 @@
     size = width * width
     for s in range(slots):
 
-        def side_turn(side, carry):
+        sides = []
+        for side in range(2):
             fresh = keep_ref[s] * state_ref[s, side] + (
                 (1.0 - decay_rate) * clip * clip) * next_ref[s, side]
             next_ref[s, side] = fresh
-            roots[side] = inverse_root(fresh)
-            return carry
-
-        lax.fori_loop(0, 2, side_turn, 0)
+            sides.append(fresh)
+        left_root, right_root = inverse_roots(sides)
         gradient = summed[s] * clip
-        precond = split_dot(halves(roots[0]), halves(gradient))
-        precond = split_dot(halves(precond), halves(roots[1]))
+        precond = split_dot(halves(left_root), halves(gradient))
+        precond = split_dot(halves(precond), halves(right_root))
         target = jnp.sqrt(squares[s] * clip * clip / size + tiny_offset)
         actual = jnp.sqrt(total_of(precond * precond) / size + tiny_offset)
         finished[s] = (precond * (target / actual)).astype(jnp.bfloat16)
@@ -251,7 +253,7 @@
         out_specs=(pl.BlockSpec(memory_space=pl.ANY), pl.BlockSpec(memory_space=vmem)),
         scratch_shapes=[
             vmem((slots, width, width), bf16), vmem((slots, n - 1, width, width), bf16),
-            vmem((slots, width, width), f32), vmem((2, width, width), f32),
+            vmem((slots, width, width), f32),
             vmem((slots, width, width), bf16),
             vmem((8, 128), f32), vmem((n - 1, 8, 128), f32),
             vmem((8, 128), f32), vmem((n_mp - 1, 8, 128), f32),

time: 209 us -> 207 us (level)
  no operation moved by 1% of the time
where the time goes in v3:
time: 207 us
  Pallas kernels  197 us (95%)
  local copies, waits for them, and re-layouts  5.23 us (3%)
  other arithmetic  3.91 us (2%)
    pallas_call x1, Pallas kernels, shards(): pl.pallas_call(functools.partial(step_kernel, n, n_mp, entries), out_shap...  176 us
    pallas_call x2, Pallas kernels, placed(): pl.pallas_call(place_kernel, out_shape=jax.ShapeDtypeStruct((count,) + sh...  20.7 us
    unnamed x3, local copies, waits for them, and re-layouts  4.64 us

profile of v3, /device:TPU:0, one launch (start us, length us, event | category | flops | bytes accessed | tf_op | source)
XLA Modules:
  0.0 206.9 jit_solution(4148688608586763712)
XLA Ops:
  0.6 0.9 convert_reduce_fusion
  1.5 0.7 fusion.2
  2.2 0.1 fusion
  2.3 0.6 dynamic-slice_select_fusion.keep_ref
  2.9 0.5 convert_element_type.7.valid_ref
  3.4 0.6 select_reduce_fusion.index_ref
  4.0 12.1 %shard_map.50 = bf16[16,512,512]{2,1,0:T(8,128)(2,1)} custom-call(s32[16]{0:T(128)} %select_reduce_fusion.index_ref, s32[16]{0:T(128)} %convert_element_type.7.valid_ref, bf16[10,512,512]{2,1,0:T(8,128)(2,1)} %bitcast.15), custom_call_target="tpu_custom_call" | custom-call | bytes 16777216 | tf_op jit(solution)/shard_map/pallas_call | solution.py:210
  16.2 0.0 copy-start
  16.2 176.4 %shard_map.51 = (bf16[8,2,512,512]{3,2,1,0:T(8,128)(2,1)}, f32[2,2,512,512]{3,2,1,0:T(8,128)}) custom-call(f32[2]{0:T(128)} %dynamic-slice_select_fusion.keep_ref, bf16[8,2,512,512]{3,2,1,0:T(8,128)(2,1)} %bitcast.13, f32[2,2,512,512]{3,2,1,0:T(8,128)} %bitcast.16), custom_call_target="tpu_custom_call" | custom-call | tf_op jit(solution)/shard_map/pallas_call | solution.py:247
  192.6 0.0 copy-done
  192.6 0.5 multiply_add_fusion.index_ref
  193.1 0.6 broadcast_2_valid_ref.2.valid_ref
  193.7 8.6 %shard_map.52 = bf16[10,512,512]{2,1,0:T(8,128)(2,1)} custom-call(s32[10]{0:T(128)} %multiply_add_fusion.index_ref, s32[10]{0:T(128)} %broadcast_2_valid_ref.2.valid_ref, bf16[16,512,512]{2,1,0:T(8,128)(2,1)} %bitcast.14), custom_call_target="tpu_custom_call" | custom-call | bytes 10485760 | tf_op jit(solution)/shard_map/pallas_call | solution.py:210
  202.3 4.6 %copy.6 = f32[1,1,2,2,512,512]{5,4,3,2,1,0:T(8,128)} copy(f32[1,1,2,2,512,512]{5,4,3,2,1,0:T(8,128)} %bitcast.17) | data formatting | bytes 8388608
Async XLA Ops:
  16.2 176.4 %copy-start = (s32[1,10]{1,0:T(1,128)S(1)}, s32[1,10]{1,0:T(1,128)}, u32[]{:S(2)}) copy-start(s32[1,10]{1,0:T(1,128)} %param.5) | copy-start | bytes 124
